TPU v7x, 32 devices: a whole 2x2x4 slice. The times are simulated.
32 devices in a mesh: groups: 2 (over y), expert: 4 (over z), tensor: 2 (over x), seq: 2 (over core).
Axes of the slice: x: 2, y: 2, z: 4, core: 2. Of those that a mesh axis runs over, the one named last changes fastest.
Arguments:
- tokens: bfloat16 [4096, 4096], P(('groups', 'expert', 'seq'), 'tensor'), parts along dimension 0, may hold values from -6 to 6
- gate_values: float32 [4096, 2], P(('groups', 'expert', 'seq')), parts along dimension 0, may hold values from 0.2 to 1.2
- routes: int32 [4096, 2], P(('groups', 'expert', 'seq')), parts along dimension 0, may hold values from 0 to 3, all different within a row; in each aligned block of 256 rows (0 to 255, 256 to 511, ...) at most 192 rows name the same one
- w_down: bfloat16 [4096, 1024], P('tensor'), may hold values from -0.09375 to 0.09375
- expert_gate: bfloat16 [4, 1024, 2048], P('expert', None, 'tensor'), may hold values from -0.1875 to 0.1875
- expert_up: bfloat16 [4, 1024, 2048], P('expert', None, 'tensor'), may hold values from -0.1875 to 0.1875
- expert_down: bfloat16 [4, 2048, 1024], P('expert', 'tensor'), may hold values from -0.125 to 0.125
- w_up: bfloat16 [1024, 4096], P(None, 'tensor'), may hold values from -0.1875 to 0.1875
Outputs:
- layer_out: bfloat16 [4096, 4096], P(('groups', 'expert', 'seq'), 'tensor'), parts along dimension 0
There are 2 independent parts, one for each index of `groups`. A program takes and returns all parts, laid end to end along the dimension named above; an argument that names none is the same for every part. Nothing has to cross between parts.
Inputs may be any that keep to these rules, and one draw needn't show every extreme that they name: `routes`: in the 256 rows of one device no expert is named by more than 192 pairs, and one expert is named by exactly 192; a row names 2 different experts.
All inputs are finite; a program needn't handle non-finite values.
Results may differ from a plain program's by a relative error of at most 0.014.
Values may be sent and summed in bfloat16 or wider, within the bound.
A program may use at most 64 MiB of HBM per device.

v0:
```python
import jax
import jax.numpy as jnp
from jax import lax
from jax.sharding import PartitionSpec as P


def local(tokens, gate_values, routes, w_down, expert_gate, expert_up, expert_down, w_up):
    tok_rows, top_count = routes.shape
    lat_width = w_down.shape[1]
    n_expert = lax.axis_size("expert")
    n_tensor = lax.axis_size("tensor")
    exp_dev = expert_gate.shape[0]
    experts_all = n_expert * exp_dev
    capacity = n_tensor * (
        (3 * tok_rows * top_count + 2 * experts_all * n_tensor - 1) // (2 * experts_all * n_tensor)
    )
    partial_value = jnp.dot(tokens, w_down, preferred_element_type=jnp.float32)
    latent = lax.psum(partial_value, "tensor").astype(jnp.bfloat16)
    chosen = routes.reshape(-1)
    onehot = (chosen[:, None] == jnp.arange(experts_all, dtype=jnp.int32)[None, :]).astype(
        jnp.int32
    )
    earlier = jnp.cumsum(onehot, axis=0) - onehot
    slot_pos = jnp.sum(earlier * onehot, axis=1)
    flat_ids = chosen * capacity + slot_pos
    token_of = jnp.arange(tok_rows * top_count, dtype=jnp.int32) // top_count
    outbox = (
        jnp.zeros((experts_all * capacity, lat_width), jnp.bfloat16)
        .at[flat_ids]
        .set(latent[token_of])
    )
    outbox = outbox.reshape(n_expert, exp_dev, capacity, lat_width)
    inbox = lax.all_to_all(outbox, "expert", split_axis=0, concat_axis=0, tiled=True)
    gate_act = jnp.einsum("sicl,ilf->sicf", inbox, expert_gate, preferred_element_type=jnp.float32)
    up_act = jnp.einsum("sicl,ilf->sicf", inbox, expert_up, preferred_element_type=jnp.float32)
    hidden = (jax.nn.silu(gate_act) * up_act).astype(jnp.bfloat16)
    expert_out = jnp.einsum(
        "sicf,ifl->sicl", hidden, expert_down, preferred_element_type=jnp.float32
    )
    weights = gate_values.reshape(-1)
    returned = lax.all_to_all(
        expert_out.astype(jnp.bfloat16), "expert", split_axis=0, concat_axis=0, tiled=True
    ).astype(expert_out.dtype)
    picked = returned.reshape(-1, lat_width)[flat_ids]
    partial_out = (picked * weights[:, None]).reshape(tok_rows, top_count, lat_width).sum(axis=1)
    combined = lax.psum(partial_out.astype(jnp.bfloat16), "tensor")
    return jnp.dot(combined, w_up, preferred_element_type=jnp.float32).astype(jnp.bfloat16)


def solution(mesh):
    return jax.shard_map(
        local,
        mesh=mesh,
        in_specs=(
            P(("groups", "expert", "seq"), "tensor"),
            P(("groups", "expert", "seq"), None),
            P(("groups", "expert", "seq"), None),
            P("tensor", None),
            P("expert", None, "tensor"),
            P("expert", None, "tensor"),
            P("expert", "tensor", None),
            P(None, "tensor"),
        ),
        out_specs=P(("groups", "expert", "seq"), "tensor"),
        check_vma=False,
    )
```

profile of v0, /device:TPU:0, one launch (start us, length us, event | category | flops | bytes accessed | tf_op | source)
XLA Modules:
  0.0 203.2 jit_solution(781375774663681222)
XLA Ops:
  6.5 1.0 copy.15
  7.5 0.1 eq.29
  7.6 0.1 eq.25
  7.8 0.7 broadcast_multiply_fusion
  8.5 1.2 reduce-window.6
  9.7 0.2 slice_reduce_fusion
  9.9 0.2 reduce-window.9
  10.2 0.1 copy.14
  10.3 0.1 mul.37
  10.5 3.8 %fusion.38 = f32[256,1024]{1,0:T(8,128)S(1)} fusion(bf16[256,2048]{1,0:T(8,128)(2,1)} %param.8, bf16[2048,1024]{1,0:T(8,128)(2,1)} %param.11), kind=kOutput, calls=%fused_computation.46 | convolution fusion | flops 1073741824 | bytes 6291456 | tf_op jit(solution)/shard_map/dot_general | solution.py:17
  14.3 30.9 %all-reduce.4 = bf16[256,1024]{1,0:T(8,128)(2,1)} all-reduce(f32[256,1024]{1,0:T(8,128)S(1)} %fusion.38), channel_id=1, replica_groups=mesh['groups'=2,'expert'=4,'tensor'=2,'seq'=2] {'tensor'}, use_global_device_ids=true, to_apply=%region_3.4 | all-reduce | flops 262144 | bytes 1572864 | tf_op jit(solution)/shard_map/psum | solution.py:18
  45.2 8.3 %scatter_custom_fusion = bf16[768,1024]{1,0:T(8,128)(2,1)} fusion(s32[512]{0:T(512)S(1)} %bitcast.108, bf16[256,1024]{1,0:T(8,128)(2,1)} %all-reduce.4, s32[1024]{0:T(1024)S(1)} %pad_clamp_fusion.1, bf16[]{:T(256)} %constant.26.clone.1), kind=kCustom, calls=%fused_computation.24 | custom fusion | bytes 1573376 | tf_op jit(solution)/shard_map/scatter | solution.py:30
  53.4 40.3 %all_to_all.10 = bf16[4,1,192,1024]{3,2,1,0:T(8,128)(2,1)S(1)} all-to-all(bf16[4,1,192,1024]{3,2,1,0:T(8,128)(2,1)} %bitcast.107), channel_id=1, replica_groups=mesh['groups'=2,'expert'=4,'tensor'=2,'seq'=2] {'expert'}, dimensions={0} | all-to-all | bytes 3145728 | tf_op jit(solution)/shard_map/all_to_all | solution.py:33
  93.7 1.2 copy-done.1
  94.9 3.5 %fusion.6 = f32[4,192,1024]{2,1,0:T(8,128)} fusion(bf16[1,1024,1024]{2,1,0:T(8,128)(2,1)S(1)} %copy-done, bf16[4,1,192,1024]{3,2,1,0:T(8,128)(2,1)S(1)} %all_to_all.10), kind=kOutput, calls=%fused_computation.13 | convolution fusion | flops 1610612736 | bytes 6815744 | tf_op jit(solution)/shard_map/sicl,ilf->sicf/dot_general | solution.py:35
  98.4 8.4 %fusion.17 = bf16[4,1,192,1024]{3,2,1,0:T(8,128)(2,1)} fusion(bf16[1,1024,1024]{2,1,0:T(8,128)(2,1)} %param.14, f32[4,192,1024]{2,1,0:T(8,128)} %fusion.6, bf16[1,1024,1024]{2,1,0:T(8,128)(2,1)} %param.12, bf16[4,1,192,1024]{3,2,1,0:T(8,128)(2,1)} %copy-done.1), kind=kOutput, calls=%fused_computation.23 | convolution fusion | flops 3226730496 | bytes 10485760 | tf_op jit(solution)/shard_map/sicf,ifl->sicl/dot_general | solution.py:37
  106.8 4.5 %all-to-all-start.1 = ((bf16[4,1,192,1024]{3,2,1,0:T(8,128)(2,1)}), bf16[4,1,192,1024]{3,2,1,0:T(8,128)(2,1)}, u32[]{:S(2)}, u32[]{:S(2)}) async-start(bf16[4,1,192,1024]{3,2,1,0:T(8,128)(2,1)} %fusion.17), calls=%async_computation.1 | async-start | bytes 3145728 | tf_op jit(solution)/shard_map/all_to_all | solution.py:41
  111.5 35.7 %all-to-all-done.1 = bf16[4,1,192,1024]{3,2,1,0:T(8,128)(2,1)} async-done(((bf16[4,1,192,1024]{3,2,1,0:T(8,128)(2,1)}), bf16[4,1,192,1024]{3,2,1,0:T(8,128)(2,1)}, u32[]{:S(2)}, u32[]{:S(2)}) %all-to-all-start.1) | async-done | bytes 1572896 | tf_op jit(solution)/shard_map/all_to_all | solution.py:41
  147.2 3.5 %bitcast_convert_fusion = f32[768,1024]{1,0:T(8,128)} fusion(bf16[4,1,192,1024]{3,2,1,0:T(8,128)(2,1)} %all-to-all-done.1), kind=kLoop, calls=%fused_computation.19 | loop fusion | flops 786432 | bytes 4718592 | tf_op jit(solution)/shard_map/reshape | solution.py:44
  150.7 5.5 %gather_fusion = f32[512,1024]{1,0:T(8,128)} fusion(f32[768,1024]{1,0:T(8,128)} %bitcast_convert_fusion, s32[1024]{0:T(1024)S(1)} %pad_clamp_fusion), kind=kCustom, calls=%fused_computation.1 | custom fusion | bytes 4196352 | tf_op jit(solution)/shard_map/gather | solution.py:44
  156.2 3.5 %gather.10 = f32[256,2,1024]{2,1,0:T(2,128)} reshape(f32[512,1024]{1,0:T(8,128)} %gather_fusion) | data formatting | bytes 4194304 | tf_op jit(solution)/shard_map/gather | solution.py:44
  159.7 5.1 %multiply_reduce_fusion = bf16[256,1024]{1,0:T(8,128)(2,1)} fusion(f32[256,2,1024]{2,1,0:T(2,128)} %gather.10, f32[256,2]{1,0:T(8,128)S(1)} %copy.18), kind=kLoop, calls=%fused_computation.17 | loop fusion | flops 786432 | bytes 2623488 | tf_op jit(solution)/shard_map/reduce_sum | solution.py:45
  164.8 26.9 %all-reduce.3.cloned.1.call-done = bf16[256,1024]{1,0:T(8,128)(2,1)} async-done(((bf16[256,1024]{1,0:T(8,128)(2,1)}), bf16[256,1024]{1,0:T(8,128)(2,1)}) %all-reduce.3.cloned.1.call-update) | async-done | bytes 524304 | tf_op jit(solution)/shard_map/psum | solution.py:46
  191.8 4.6 %convolution_convert_fusion = bf16[256,2048]{1,0:T(8,128)(2,1)} fusion(bf16[256,1024]{1,0:T(8,128)(2,1)} %all-reduce.3.cloned.1.call-done, bf16[1024,2048]{1,0:T(8,128)(2,1)} %param.15), kind=kOutput, calls=%fused_computation.10 | convolution fusion | flops 1074266112 | bytes 5767168 | tf_op jit(solution)/shard_map/dot_general | solution.py:47
  (15 shorter events, 0.3 us)
Async XLA Ops:
  6.5 88.4 %copy-start = (bf16[1,1024,1024]{2,1,0:T(8,128)(2,1)S(1)}, bf16[1,1024,1024]{2,1,0:T(8,128)(2,1)}, u32[]{:S(2)}) copy-start(bf16[1,1024,1024]{2,1,0:T(8,128)(2,1)} %param.13) | copy-start | bytes 6291460
  93.7 1.2 copy-start.1
  106.8 4.6 %copy-start.2 = (f32[256,2]{0,1:T(2,128)S(1)}, f32[256,2]{0,1:T(2,128)}, u32[]{:S(2)}) copy-start(f32[256,2]{0,1:T(2,128)} %param.9) | copy-start | bytes 6148
  106.8 40.4 %all-to-all-start.1 = ((bf16[4,1,192,1024]{3,2,1,0:T(8,128)(2,1)}), bf16[4,1,192,1024]{3,2,1,0:T(8,128)(2,1)}, u32[]{:S(2)}, u32[]{:S(2)}) async-start(bf16[4,1,192,1024]{3,2,1,0:T(8,128)(2,1)} %fusion.17), calls=%async_computation.1 | async-start | bytes 3145728 | tf_op jit(solution)/shard_map/all_to_all | solution.py:41
  111.3 80.4 %all-reduce.3.cloned.1.call-start = ((), (), s32[]{:S(2)}) async-start(), calls=%async_computation.2 | async-start | bytes 1048576 | tf_op jit(solution)/shard_map/psum | solution.py:46
Sparse Core Ops, SparseCore 0:
  165.0 26.7 all-reduce.2
where the time goes:
time: 204 us; the launch traced here: 203 us
  blocking collectives  71.2 us (35%)
  waiting for transfers between devices  62.6 us (31%)
  local copies, waits for them, and re-layouts  20.3 us (10%)
  matrix products  20.3 us (10%)
  between operations  13.5 us (7%)
  other arithmetic  10.8 us (5%)
  starting transfers between devices  4.53 us (2%)
    all_to_all x1, blocking collectives, local(): lax.all_to_all(outbox, 'expert', split_axis=0, concat_axis=0, tiled=True)  40.3 us
    all_to_all x1, waiting for transfers between devices, local(): lax.all_to_all(expert_out.astype(jnp.bfloat16), 'expert', split_axis=0, c...  35.7 us
    psum x1, blocking collectives, local(): latent = lax.psum(partial_value, 'tensor').astype(jnp.bfloat16)  30.9 us
    psum x1, waiting for transfers between devices, local(): combined = lax.psum(partial_out.astype(jnp.bfloat16), 'tensor')  26.9 us
    gather x2, local copies, waits for them, and re-layouts, local(): picked = returned.reshape(-1, lat_width)[flat_ids]  9 us
    dot_general x1, matrix products, local(): jnp.einsum('sicf,ifl->sicl', hidden, expert_down, preferred_element_type=...  8.43 us
    scatter x1, local copies, waits for them, and re-layouts, local(): outbox = jnp.zeros((experts_all * capacity, lat_width), jnp.bfloat16).at[...  8.25 us
    reduce_sum x1, other arithmetic, local(): (picked * weights[:, None]).reshape(tok_rows, top_count, lat_width)  5.13 us
  transfers between devices with their start and end apart: 2, of which 2 were waited for; matrix products, arithmetic and copies ran while one was open for 0% of the time, Pallas kernels for 0%

commit v1 on v0

v1 whole, which is shorter than its diff:
```python
import functools

import jax
import jax.numpy as jnp
from jax import lax
from jax.experimental import pallas as pl
from jax.experimental.pallas import tpu as pltpu
from jax.sharding import PartitionSpec as P

MESH = pl.DeviceIdType.MESH
F32 = jnp.float32
BF16 = jnp.bfloat16


def flip(index, step, count):
    out, bit = 0, 1
    while bit < count:
        out = out + ((index // bit + (step // bit) % 2) % 2) * bit
        bit *= 2
    return out


def kernel(
    n_exp, n_ten, cap,
    tokens, gates, routes, w_down, w_gate, w_upx, w_dn, w_up, out,
    tok_v, wd_v, wg_v, wu_v, wdn_v, wup_v,
    lat_send, lat_recv, outbox, inbox, o_own, o_send, o_recv, r_send, r_recv, comb, acc, out_v,
    load_sem, rs_s, rs_r, z_s, z_r, ag_s, ag_r, os_s, os_r, rt_s, rt_r, fa_s, fa_r, st_sem,
):
    me = lax.axis_index("expert")
    ten = lax.axis_index("tensor")
    rows = tok_v.shape[0]
    lat = wd_v.shape[1]
    lw = lat // n_ten

    def cols(t):
        return pl.ds(pl.multiple_of(t * lw, 128), lw)

    mine = cols(ten)

    loads = []
    for i, (src, dst) in enumerate(
        ((tokens, tok_v), (w_down, wd_v), (w_gate.at[0], wg_v), (w_upx.at[0], wu_v), (w_dn.at[0], wdn_v), (w_up, wup_v))
    ):
        c = pltpu.make_async_copy(src, dst, load_sem.at[i])
        c.start()
        loads.append(c)

    barrier = pltpu.get_barrier_semaphore()
    for k in range(1, n_exp):
        pl.semaphore_signal(barrier, inc=1, device_id={"expert": flip(me, k, n_exp)}, device_id_type=MESH)
    for j in range(1, n_ten):
        pl.semaphore_signal(barrier, inc=1, device_id={"tensor": (ten + j) % n_ten}, device_id_type=MESH)

    lanes = 128
    ids = lax.broadcasted_iota(jnp.int32, (rows, lanes), 1)
    first, second = routes[:, 0:1], routes[:, 1:2]
    named = jnp.where((first == ids) | (second == ids), 1.0, 0.0).astype(F32)
    r0 = lax.broadcasted_iota(jnp.int32, (rows, rows), 0)
    r1 = lax.broadcasted_iota(jnp.int32, (rows, rows), 1)
    below = jnp.where(r1 < r0, 1.0, 0.0).astype(BF16)
    slot = jnp.dot(below, named.astype(BF16), preferred_element_type=F32)
    code = jnp.where(named > 0.5, slot, -1.0)
    code_t = code.T
    sub = lax.broadcasted_iota(jnp.int32, (lanes, rows), 0)

    def select_rows(e):
        line = jnp.sum(jnp.where(sub == e, code_t, 0.0), axis=0, keepdims=True)
        at = lax.broadcasted_iota(jnp.int32, (cap, rows), 0).astype(F32)
        return jnp.where(at == line, 1.0, 0.0).astype(BF16)

    def place_rows(e):
        line = jnp.sum(jnp.where(ids == e, code, 0.0), axis=1, keepdims=True)
        at = lax.broadcasted_iota(jnp.int32, (rows, cap), 1).astype(F32)
        return jnp.where(at == line, 1.0, 0.0).astype(BF16)

    def weight(e):
        return jnp.where(first == e, gates[:, 0:1], 0.0) + jnp.where(second == e, gates[:, 1:2], 0.0)

    pl.semaphore_wait(barrier, n_exp - 1 + n_ten - 1)

    loads[0].wait()
    loads[1].wait()

    def remote(src, dst, s, r, to):
        return pltpu.make_async_remote_copy(
            src_ref=src, dst_ref=dst, send_sem=s, recv_sem=r, device_id=to, device_id_type=MESH
        )

    rs = {}
    for j in range(1, n_ten):
        to = (ten + j) % n_ten
        lat_send[j] = jnp.dot(tok_v[...], wd_v[:, cols(to)], preferred_element_type=F32).astype(BF16)
        rs[j] = remote(lat_send.at[j], lat_recv.at[j], rs_s.at[j], rs_r.at[j], {"tensor": to})
        rs[j].start()
    total = jnp.dot(tok_v[...], wd_v[:, mine], preferred_element_type=F32)
    for j in range(1, n_ten):
        rs[j].wait()
        total = total + lat_recv[j].astype(F32)
    latent = total.astype(BF16)

    order = list(range(n_exp // 2, n_exp)) + list(range(n_exp // 2 - 1, 0, -1))
    z, ag, osd, rt = {}, {}, {}, {}

    def gather(k):
        for j in range(1, n_ten):
            to = (ten + j) % n_ten
            here = inbox.at[k, :, mine]
            ag[k, j] = remote(here, here, ag_s.at[k, j], ag_r.at[k, j], {"tensor": to})
            ag[k, j].start()

    for k in order:
        e = flip(me, k, n_exp)
        outbox[k] = jnp.dot(select_rows(e), latent, preferred_element_type=F32).astype(BF16)
        z[k] = remote(outbox.at[k], inbox.at[k, :, mine], z_s.at[k], z_r.at[k], {"expert": e})
        z[k].start()
    inbox[0, :, mine] = jnp.dot(select_rows(me), latent, preferred_element_type=F32).astype(BF16)
    gather(0)

    for i in range(2, 5):
        loads[i].wait()

    def stage_a(k):
        z[k].wait()
        gather(k)

    def stage_b(k):
        for j in range(1, n_ten):
            ag[k, j].wait()
        x = inbox[k]
        g = jnp.dot(x, wg_v[...], preferred_element_type=F32)
        u = jnp.dot(x, wu_v[...], preferred_element_type=F32)
        h = (g / (1.0 + jnp.exp(-g)) * u).astype(BF16)
        for j in range(1, n_ten):
            to = (ten + j) % n_ten
            o_send[k, j] = jnp.dot(h, wdn_v[:, cols(to)], preferred_element_type=F32).astype(BF16)
            osd[k, j] = remote(o_send.at[k, j], o_recv.at[k, j], os_s.at[k, j], os_r.at[k, j], {"tensor": to})
            osd[k, j].start()
        o_own[k] = jnp.dot(h, wdn_v[:, mine], preferred_element_type=F32)

    def stage_c(k):
        y = o_own[k]
        for j in range(1, n_ten):
            osd[k, j].wait()
            y = y + o_recv[k, j].astype(F32)
        if k == 0:
            r_recv[0] = y.astype(BF16)
            return
        r_send[k] = y.astype(BF16)
        rt[k] = remote(r_send.at[k], r_recv.at[k], rt_s.at[k], rt_r.at[k], {"expert": flip(me, k, n_exp)})
        rt[k].start()

    line = [0] + order
    stage_b(0)
    for i in range(1, n_exp):
        stage_a(line[i])
        stage_c(line[i - 1])
        stage_b(line[i])
    stage_c(line[-1])

    both = jnp.zeros((rows, lw), F32)
    for k in line:
        e = flip(me, k, n_exp)
        if k:
            rt[k].wait()
        both = both + weight(e) * jnp.dot(place_rows(e), r_recv[k], preferred_element_type=F32)
    comb[:, mine] = both.astype(BF16)
    fa = {}
    for j in range(1, n_ten):
        to = (ten + j) % n_ten
        fa[j] = remote(comb.at[:, mine], comb.at[:, mine], fa_s.at[j], fa_r.at[j], {"tensor": to})
        fa[j].start()
    loads[5].wait()

    def up_rows(t):
        return pl.ds(pl.multiple_of(t * lw, 128), lw)

    acc[...] = jnp.dot(comb[:, mine], wup_v[up_rows(ten), :], preferred_element_type=F32)
    for j in range(1, n_ten):
        fa[j].wait()
    width = out_v.shape[1]
    parts = 2 if width >= 512 else 1
    pw = width // parts
    stores = []
    for p in range(parts):
        span = slice(p * pw, (p + 1) * pw)
        y = acc[:, span]
        for j in range(1, n_ten):
            t = (ten + n_ten - j) % n_ten
            y = y + jnp.dot(comb[:, cols(t)], wup_v[up_rows(t), span], preferred_element_type=F32)
        out_v[:, span] = y.astype(BF16)
        c = pltpu.make_async_copy(out_v.at[:, span], out.at[:, span], st_sem.at[p])
        c.start()
        stores.append(c)
    for c in stores:
        c.wait()


def local(tokens, gate_values, routes, w_down, expert_gate, expert_up, expert_down, w_up):
    rows, top = routes.shape
    lat = w_down.shape[1]
    n_exp = lax.axis_size("expert")
    n_ten = lax.axis_size("tensor")
    exp_dev = expert_gate.shape[0]
    total = n_exp * exp_dev
    cap = n_ten * ((3 * rows * top + 2 * total * n_ten - 1) // (2 * total * n_ten))
    lw = lat // n_ten
    width = w_up.shape[1]
    dma = pltpu.SemaphoreType.DMA
    any_spec = pl.BlockSpec(memory_space=pl.ANY)
    vmem = pl.BlockSpec(memory_space=pltpu.VMEM)
    return pl.pallas_call(
        functools.partial(kernel, n_exp, n_ten, cap),
        out_shape=jax.ShapeDtypeStruct((rows, width), BF16),
        in_specs=[any_spec, vmem, vmem] + [any_spec] * 5,
        out_specs=any_spec,
        scratch_shapes=[
            pltpu.VMEM(tokens.shape, BF16),
            pltpu.VMEM(w_down.shape, BF16),
            pltpu.VMEM(expert_gate.shape[1:], BF16),
            pltpu.VMEM(expert_up.shape[1:], BF16),
            pltpu.VMEM(expert_down.shape[1:], BF16),
            pltpu.VMEM(w_up.shape, BF16),
            pltpu.VMEM((n_ten, rows, lw), BF16),
            pltpu.VMEM((n_ten, rows, lw), BF16),
            pltpu.VMEM((n_exp, cap, lw), BF16),
            pltpu.VMEM((n_exp, cap, lat), BF16),
            pltpu.VMEM((n_exp, cap, lw), F32),
            pltpu.VMEM((n_exp, n_ten, cap, lw), BF16),
            pltpu.VMEM((n_exp, n_ten, cap, lw), BF16),
            pltpu.VMEM((n_exp, cap, lw), BF16),
            pltpu.VMEM((n_exp, cap, lw), BF16),
            pltpu.VMEM((rows, lat), BF16),
            pltpu.VMEM((rows, width), F32),
            pltpu.VMEM((rows, width), BF16),
            dma((6,)),
            dma((n_ten,)), dma((n_ten,)),
            dma((n_exp,)), dma((n_exp,)),
            dma((n_exp, n_ten)), dma((n_exp, n_ten)),
            dma((n_exp, n_ten)), dma((n_exp, n_ten)),
            dma((n_exp,)), dma((n_exp,)),
            dma((n_ten,)), dma((n_ten,)),
            dma((2,)),
        ],
        compiler_params=pltpu.CompilerParams(
            collective_id=0, has_side_effects=True, vmem_limit_bytes=56 * 1024 * 1024
        ),
        name="moe_layer",
    )(tokens, gate_values, routes, w_down, expert_gate, expert_up, expert_down, w_up)


def solution(mesh):
    return jax.shard_map(
        local,
        mesh=mesh,
        in_specs=(
            P(("groups", "expert", "seq"), "tensor"),
            P(("groups", "expert", "seq"), None),
            P(("groups", "expert", "seq"), None),
            P("tensor", None),
            P("expert", None, "tensor"),
            P("expert", None, "tensor"),
            P("expert", "tensor", None),
            P(None, "tensor"),
        ),
        out_specs=P(("groups", "expert", "seq"), "tensor"),
        check_vma=False,
    )
```

time: 204 us -> 76.1 us (0.37)
  blocking collectives: 71.2 us -> 0 us
  Pallas kernels: 0 us -> 70.6 us
  waiting for transfers between devices: 62.6 us -> 0 us
  matrix products: 20.3 us -> 0 us
  local copies, waits for them, and re-layouts: 20.3 us -> 5.24 us
  between operations: 13.5 us -> 0.01 us
  other arithmetic: 10.8 us -> 0 us
  starting transfers between devices: 4.53 us -> 0 us
    pallas_call x0 -> x1, Pallas kernels: none -> 70.6 us  [local(): pl.pallas_call(functools.partial(kernel, n_exp, n_ten, cap), out_shape=ja...]
    all_to_all x1 -> x0, blocking collectives: 40.3 us -> none  [local(): lax.all_to_all(outbox, 'expert', split_axis=0, concat_axis=0, tiled=True)]
    all_to_all x1 -> x0, waiting for transfers between devices: 35.7 us -> none  [local(): lax.all_to_all(expert_out.astype(jnp.bfloat16), 'expert', split_axis=0, c...]
    psum x1 -> x0, blocking collectives: 30.9 us -> none  [local(): latent = lax.psum(partial_value, 'tensor').astype(jnp.bfloat16)]
    psum x1 -> x0, waiting for transfers between devices: 26.9 us -> none  [local(): combined = lax.psum(partial_out.astype(jnp.bfloat16), 'tensor')]
    dot_general x4 -> x0, matrix products: 20.3 us -> none  [the longest x1 8.43 us: local(): jnp.einsum('sicf,ifl->sicl', hidden, expert_down, preferred_element_type=...]
    gather x2 -> x0, local copies, waits for them, and re-layouts: 9 us -> none  [local(): picked = returned.reshape(-1, lat_width)[flat_ids]]
    scatter x1 -> x0, local copies, waits for them, and re-layouts: 8.25 us -> none  [local(): outbox = jnp.zeros((experts_all * capacity, lat_width), jnp.bfloat16).at[...]
  transfers between devices with their start and end apart: 2 -> 0, of which waited for: 2 -> 0; matrix products, arithmetic and copies ran while one was open for 0% -> 0% of each run, Pallas kernels for 0% -> 0%
where the time goes in v1:
time: 76.1 us; the launch traced here: 75.9 us
  Pallas kernels  70.6 us (93%)
  local copies, waits for them, and re-layouts  5.24 us (7%)
    pallas_call x1, Pallas kernels, local(): pl.pallas_call(functools.partial(kernel, n_exp, n_ten, cap), out_shape=ja...  70.6 us
    unnamed x3, local copies, waits for them, and re-layouts  5.24 us

profile of v1, /device:TPU:0, one launch (start us, length us, event | category | flops | bytes accessed | tf_op | source)
XLA Modules:
  0.0 75.9 jit_solution(17918821220414408885)
XLA Ops:
  0.0 1.5 %copy.9.gates = f32[256,2]{1,0:T(8,128)} copy(f32[256,2]{0,1:T(2,128)} %param.9) | data formatting | bytes 4096 | tf_op args[1]
  1.5 1.5 %copy.10.routes = s32[256,2]{1,0:T(8,128)} copy(s32[256,2]{0,1:T(2,128)} %param.10) | data formatting | bytes 4096 | tf_op args[2]
  2.9 70.6 %moe_layer.1 = bf16[256,2048]{1,0:T(8,128)(2,1)} custom-call(bf16[256,2048]{1,0:T(8,128)(2,1)} %tokens.1, f32[256,2]{1,0:T(8,128)} %copy.9.gates, s32[256,2]{1,0:T(8,128)} %copy.10.routes, bf16[2048,1024]{1,0:T(8,128)(2,1)} %w_down.1, bf16[1,1024,1024]{2,1,0:T(8,128)(2,1)} %w_gate.1, bf16[1,1024,1024]{2,1,0:T(8,128)(2,1)} %w_upx.1, ...), custom_call_target="tpu_custom_call" | custom-call | tf_op jit(solution)/shard_map/moe_layer/pallas_call | solution.py:212
  73.6 2.3 %copy.12 = bf16[256,2048]{1,0:T(8,128)(2,1)} copy(bf16[256,2048]{1,0:T(8,128)(2,1)} %moe_layer.1) | data formatting | bytes 2097152

commit v2 on v1

--- a/solution.py
+++ b/solution.py
@@ -38,13 +38,14 @@
 
     mine = cols(ten)
 
-    loads = []
-    for i, (src, dst) in enumerate(
-        ((tokens, tok_v), (w_down, wd_v), (w_gate.at[0], wg_v), (w_upx.at[0], wu_v), (w_dn.at[0], wdn_v), (w_up, wup_v))
-    ):
+    def load(i, src, dst):
         c = pltpu.make_async_copy(src, dst, load_sem.at[i])
         c.start()
-        loads.append(c)
+        return c
+
+    peers = [(ten + j) % n_ten for j in range(1, n_ten)] + [ten]
+    load_tok = load(5, tokens, tok_v)
+    load_down = [load(6 + i, w_down.at[:, cols(t)], wd_v.at[:, cols(t)]) for i, t in enumerate(peers)]
 
     barrier = pltpu.get_barrier_semaphore()
     for k in range(1, n_exp):
@@ -54,15 +55,16 @@
 
     lanes = 128
     ids = lax.broadcasted_iota(jnp.int32, (rows, lanes), 1)
-    first, second = routes[:, 0:1], routes[:, 1:2]
-    named = jnp.where((first == ids) | (second == ids), 1.0, 0.0).astype(F32)
+    sub = lax.broadcasted_iota(jnp.int32, (lanes, rows), 0)
+    first, second = routes[0:1, :], routes[1:2, :]
+    named = jnp.where((first == sub) | (second == sub), 1.0, 0.0).astype(F32)
     r0 = lax.broadcasted_iota(jnp.int32, (rows, rows), 0)
     r1 = lax.broadcasted_iota(jnp.int32, (rows, rows), 1)
-    below = jnp.where(r1 < r0, 1.0, 0.0).astype(BF16)
-    slot = jnp.dot(below, named.astype(BF16), preferred_element_type=F32)
-    code = jnp.where(named > 0.5, slot, -1.0)
-    code_t = code.T
-    sub = lax.broadcasted_iota(jnp.int32, (lanes, rows), 0)
+    above = jnp.where(r0 < r1, 1.0, 0.0).astype(BF16)
+    slot = jnp.dot(named.astype(BF16), above, preferred_element_type=F32)
+    code_t = jnp.where(named > 0.5, slot, -1.0)
+    code = code_t.T
+    share = (jnp.where(first == sub, gates[0:1, :], 0.0) + jnp.where(second == sub, gates[1:2, :], 0.0)).T
 
     def select_rows(e):
         line = jnp.sum(jnp.where(sub == e, code_t, 0.0), axis=0, keepdims=True)
@@ -75,31 +77,36 @@
         return jnp.where(at == line, 1.0, 0.0).astype(BF16)
 
     def weight(e):
-        return jnp.where(first == e, gates[:, 0:1], 0.0) + jnp.where(second == e, gates[:, 1:2], 0.0)
-
-    pl.semaphore_wait(barrier, n_exp - 1 + n_ten - 1)
-
-    loads[0].wait()
-    loads[1].wait()
+        return jnp.sum(jnp.where(ids == e, share, 0.0), axis=1, keepdims=True)
+
+    sends = []
 
     def remote(src, dst, s, r, to):
-        return pltpu.make_async_remote_copy(
+        c = pltpu.make_async_remote_copy(
             src_ref=src, dst_ref=dst, send_sem=s, recv_sem=r, device_id=to, device_id_type=MESH
         )
-
+        c.start()
+        sends.append(c)
+        return c
+
+    load_tok.wait()
+    for j in range(1, n_ten):
+        load_down[j - 1].wait()
+        lat_send[j] = jnp.dot(tok_v[...], wd_v[:, cols(peers[j - 1])], preferred_element_type=F32).astype(BF16)
+    pl.semaphore_wait(barrier, n_exp - 1 + n_ten - 1)
     rs = {}
     for j in range(1, n_ten):
-        to = (ten + j) % n_ten
-        lat_send[j] = jnp.dot(tok_v[...], wd_v[:, cols(to)], preferred_element_type=F32).astype(BF16)
-        rs[j] = remote(lat_send.at[j], lat_recv.at[j], rs_s.at[j], rs_r.at[j], {"tensor": to})
-        rs[j].start()
+        rs[j] = remote(lat_send.at[j], lat_recv.at[j], rs_s.at[j], rs_r.at[j], {"tensor": peers[j - 1]})
+    load_down[-1].wait()
+    weights = ((w_gate.at[0], wg_v), (w_upx.at[0], wu_v), (w_dn.at[0], wdn_v), (w_up, wup_v))
+    loads = [load(i, src, dst) for i, (src, dst) in enumerate(weights)]
     total = jnp.dot(tok_v[...], wd_v[:, mine], preferred_element_type=F32)
     for j in range(1, n_ten):
-        rs[j].wait()
+        rs[j].wait_recv()
         total = total + lat_recv[j].astype(F32)
     latent = total.astype(BF16)
 
-    order = list(range(n_exp // 2, n_exp)) + list(range(n_exp // 2 - 1, 0, -1))
+    order = list(range(1,n_exp))
     z, ag, osd, rt = {}, {}, {}, {}
 
     def gather(k):
@@ -107,26 +114,31 @@
             to = (ten + j) % n_ten
             here = inbox.at[k, :, mine]
             ag[k, j] = remote(here, here, ag_s.at[k, j], ag_r.at[k, j], {"tensor": to})
-            ag[k, j].start()
+
+    late = n_exp - 1
+
+    def dispatch(k):
+        to = {"expert": flip(me, k, n_exp)}
+        z[k] = remote(outbox.at[k], inbox.at[k, :, mine], z_s.at[k], z_r.at[k], to)
 
     for k in order:
         e = flip(me, k, n_exp)
         outbox[k] = jnp.dot(select_rows(e), latent, preferred_element_type=F32).astype(BF16)
-        z[k] = remote(outbox.at[k], inbox.at[k, :, mine], z_s.at[k], z_r.at[k], {"expert": e})
-        z[k].start()
+        if k != late:
+            dispatch(k)
     inbox[0, :, mine] = jnp.dot(select_rows(me), latent, preferred_element_type=F32).astype(BF16)
     gather(0)
 
-    for i in range(2, 5):
+    for i in range(3):
         loads[i].wait()
 
     def stage_a(k):
-        z[k].wait()
+        z[k].wait_recv()
         gather(k)
 
     def stage_b(k):
         for j in range(1, n_ten):
-            ag[k, j].wait()
+            ag[k, j].wait_recv()
         x = inbox[k]
         g = jnp.dot(x, wg_v[...], preferred_element_type=F32)
         u = jnp.dot(x, wu_v[...], preferred_element_type=F32)
@@ -135,49 +147,55 @@
             to = (ten + j) % n_ten
             o_send[k, j] = jnp.dot(h, wdn_v[:, cols(to)], preferred_element_type=F32).astype(BF16)
             osd[k, j] = remote(o_send.at[k, j], o_recv.at[k, j], os_s.at[k, j], os_r.at[k, j], {"tensor": to})
-            osd[k, j].start()
         o_own[k] = jnp.dot(h, wdn_v[:, mine], preferred_element_type=F32)
 
     def stage_c(k):
         y = o_own[k]
         for j in range(1, n_ten):
-            osd[k, j].wait()
+            osd[k, j].wait_recv()
             y = y + o_recv[k, j].astype(F32)
         if k == 0:
             r_recv[0] = y.astype(BF16)
             return
         r_send[k] = y.astype(BF16)
         rt[k] = remote(r_send.at[k], r_recv.at[k], rt_s.at[k], rt_r.at[k], {"expert": flip(me, k, n_exp)})
-        rt[k].start()
+
+    both = jnp.zeros((rows, lw), F32)
+
+    def stage_d(k, both):
+        e = flip(me, k, n_exp)
+        if k:
+            rt[k].wait_recv()
+        return both + weight(e) * jnp.dot(place_rows(e), r_recv[k], preferred_element_type=F32)
 
     line = [0] + order
+    dispatch(late)
     stage_b(0)
+    stage_a(line[1])
     for i in range(1, n_exp):
-        stage_a(line[i])
+        if i + 1 < late:
+            stage_a(line[i + 1])
+        if i == late:
+            stage_a(late)
         stage_c(line[i - 1])
         stage_b(line[i])
+    both = stage_d(line[0], both)
     stage_c(line[-1])
-
-    both = jnp.zeros((rows, lw), F32)
-    for k in line:
-        e = flip(me, k, n_exp)
-        if k:
-            rt[k].wait()
-        both = both + weight(e) * jnp.dot(place_rows(e), r_recv[k], preferred_element_type=F32)
+    for k in line[1:]:
+        both = stage_d(k, both)
     comb[:, mine] = both.astype(BF16)
     fa = {}
     for j in range(1, n_ten):
         to = (ten + j) % n_ten
         fa[j] = remote(comb.at[:, mine], comb.at[:, mine], fa_s.at[j], fa_r.at[j], {"tensor": to})
-        fa[j].start()
-    loads[5].wait()
+    loads[3].wait()
 
     def up_rows(t):
         return pl.ds(pl.multiple_of(t * lw, 128), lw)
 
     acc[...] = jnp.dot(comb[:, mine], wup_v[up_rows(ten), :], preferred_element_type=F32)
     for j in range(1, n_ten):
-        fa[j].wait()
+        fa[j].wait_recv()
     width = out_v.shape[1]
     parts = 2 if width >= 512 else 1
     pw = width // parts
@@ -194,6 +212,8 @@
         stores.append(c)
     for c in stores:
         c.wait()
+    for c in sends:
+        c.wait_send()
 
 
 def local(tokens, gate_values, routes, w_down, expert_gate, expert_up, expert_down, w_up):
@@ -233,7 +253,7 @@
             pltpu.VMEM((rows, lat), BF16),
             pltpu.VMEM((rows, width), F32),
             pltpu.VMEM((rows, width), BF16),
-            dma((6,)),
+            dma((6 + n_ten,)),
             dma((n_ten,)), dma((n_ten,)),
             dma((n_exp,)), dma((n_exp,)),
             dma((n_exp, n_ten)), dma((n_exp, n_ten)),
@@ -246,7 +266,7 @@
             collective_id=0, has_side_effects=True, vmem_limit_bytes=56 * 1024 * 1024
         ),
         name="moe_layer",
-    )(tokens, gate_values, routes, w_down, expert_gate, expert_up, expert_down, w_up)
+    )(tokens, gate_values.T, routes.T, w_down, expert_gate, expert_up, expert_down, w_up)
 
 
 def solution(mesh):

time: 76.1 us -> 70.9 us (0.932)
  local copies, waits for them, and re-layouts: 5.24 us -> 2.3 us
  Pallas kernels: 70.6 us -> 68.4 us
    unnamed x3 -> x1, local copies, waits for them, and re-layouts: 5.24 us -> 2.3 us
    pallas_call x1, Pallas kernels: 70.6 us -> 68.4 us  [local(): pl.pallas_call(functools.partial(kernel, n_exp, n_ten, cap), out_shape=ja...]
where the time goes in v2:
time: 70.9 us; the launch traced here: 70.7 us
  Pallas kernels  68.4 us (96%)
  local copies, waits for them, and re-layouts  2.3 us (3%)
    pallas_call x1, Pallas kernels, local(): pl.pallas_call(functools.partial(kernel, n_exp, n_ten, cap), out_shape=ja...  68.4 us
    unnamed x1, local copies, waits for them, and re-layouts  2.3 us

profile of v2, /device:TPU:0, one launch (start us, length us, event | category | flops | bytes accessed | tf_op | source)
XLA Modules:
  0.0 70.7 jit_solution(2352676890878478556)
XLA Ops:
  0.0 68.4 %moe_layer.1 = bf16[256,2048]{1,0:T(8,128)(2,1)} custom-call(bf16[256,2048]{1,0:T(8,128)(2,1)} %tokens.1, f32[2,256]{1,0:T(2,128)} %bitcast.2, s32[2,256]{1,0:T(2,128)} %bitcast.3, bf16[2048,1024]{1,0:T(8,128)(2,1)} %w_down.1, bf16[1,1024,1024]{2,1,0:T(8,128)(2,1)} %w_gate.1, bf16[1,1024,1024]{2,1,0:T(8,128)(2,1)} %w_upx.1, bf16[1,1024,1024]{2,1,0:T(8,128)(2,1)} %w_dn.1, ...), custom_call_target="tpu_custom_call" | custom-call | tf_op jit(solution)/shard_map/moe_layer/pallas_call | solution.py:232
  68.4 2.3 %copy.10 = bf16[256,2048]{1,0:T(8,128)(2,1)} copy(bf16[256,2048]{1,0:T(8,128)(2,1)} %moe_layer.1) | data formatting | bytes 2097152
